TPU v7x, 512 devices: a whole 4x4x16 slice. The times are simulated.
512 devices in a mesh: row: 16 (over y, x), col: 32 (over z, core).
Axes of the slice: x: 4, y: 4, z: 16, core: 2. Of those that a mesh axis runs over, the one named last changes fastest.
Arguments:
- points: bfloat16 [262144, 256], P(('col', 'row')), may hold values from -6 to 6
- weights: bfloat16 [262144, 128], P(('col', 'row')), may hold values from -6 to 6
- near_blocks: int32 [2048, 16], P(('col', 'row')), may hold values from 0 to 2047, as said below
- proxies: bfloat16 [64, 256], replicated, may hold values from -6 to 6
Outputs:
- near_product: bfloat16 [262144, 128], P(('col', 'row'))
- factors: float32 [32768, 192], P(('col', 'row'))
Inputs may be any that keep to these rules, and one draw needn't show every extreme that they name: near_blocks[j, 0] = j; every entry of row j lies in the column group of j, that is in the same run of 64 blocks; entries may repeat.
All inputs are finite; a program needn't handle non-finite values.
Results may differ from a plain program's by a relative error of at most 0.01.
Values may be sent and summed in bfloat16 or wider, within the bound.
No kernel may reach another device: no remote copies, remote signals or barrier semaphores. Data moves between devices by JAX's collectives and lax.ppermute only.
A program may use at most 64 MiB of HBM per device.

v0:
```python
import jax
import jax.numpy as jnp
from jax import lax
from jax.sharding import PartitionSpec as P

DIM = 256
BLK = 128
NV = 128


def partner(value, axis, stride):
    mask = 2**stride
    pairs = [(source, source ^ mask) for source in range(lax.axis_size(axis))]
    return lax.ppermute(value, axis, pairs)


def kern_tile(left, right):
    cross = jnp.dot(left, right.T, preferred_element_type=jnp.float32)
    lnorm = jnp.sum(left.astype(jnp.float32) ** 2, axis=-1)
    rnorm = jnp.sum(right.astype(jnp.float32) ** 2, axis=-1)
    return jnp.exp(-(lnorm[:, None] + rnorm[None, :] - 2.0 * cross) * (2.0 / DIM))


def level_merge(lower_own, lower_other):
    high = lax.Precision.HIGHEST
    gram = jnp.dot(lower_own, lower_own.T, precision=high) + jnp.dot(
        lower_other, lower_other.T, precision=high
    )
    merged = jnp.linalg.cholesky(gram)
    transfer = lax.linalg.triangular_solve(merged, lower_own, left_side=True, lower=True).T
    return (merged, transfer)


def on_device(points, weights, near_blocks, proxies):
    n_local = near_blocks.shape[0]
    group_count = n_local * lax.axis_size("row")
    base = lax.axis_index("col") * group_count
    gathered = lax.all_gather(points, "row", axis=0, tiled=True)
    tblocks = gathered.reshape(group_count, BLK, DIM)
    local_ids = near_blocks - base
    sources = points.reshape(n_local, BLK, DIM)
    wblocks = weights.reshape(n_local, BLK, NV)
    targets = tblocks[local_ids]
    cross = jnp.einsum("jtad,jbd->jtab", targets, sources, preferred_element_type=jnp.float32)
    tnorm = jnp.sum(targets.astype(jnp.float32) ** 2, axis=-1)
    snorm = jnp.sum(sources.astype(jnp.float32) ** 2, axis=-1)
    dist = tnorm[:, :, :, None] + snorm[:, None, None, :] - 2.0 * cross
    tile = jnp.exp(-dist * (2.0 / DIM)).astype(jnp.bfloat16)
    contrib = jnp.einsum("jtab,jbv->jtav", tile, wblocks, preferred_element_type=jnp.float32)
    partial_value = jnp.zeros((group_count, BLK, NV), jnp.float32)
    partial_value = partial_value.at[local_ids.reshape(-1)].add(contrib.reshape(-1, BLK, NV))
    near_sum = lax.psum_scatter(
        partial_value.reshape(group_count * BLK, NV), "row", scatter_dimension=0, tiled=True
    )
    near_product = near_sum.astype(jnp.bfloat16)
    far = kern_tile(points, proxies)
    lower0 = jnp.linalg.cholesky(jnp.dot(far.T, far, precision=lax.Precision.HIGHEST))
    current = lower0
    transfers = []
    for level in range(2):
        sibling = partner(current, "col", level)
        current, transfer = level_merge(current, sibling)
        transfers.append(transfer)
    factors = jnp.concatenate([transfers[0], transfers[1], current.T], axis=1)
    return (near_product, factors)


def solution(mesh):
    placed = (P(("col", "row"), None), P(("col", "row"), None), P(("col", "row"), None), P())
    return jax.shard_map(
        on_device,
        mesh=mesh,
        in_specs=placed,
        out_specs=(P(("col", "row"), None), P(("col", "row"), None)),
        check_vma=False,
    )
```

profile of v0, /device:TPU:2, one launch (start us, length us, event | category | flops | bytes accessed | tf_op | source)
XLA Modules:
  0.0 213.1 jit_solution(5560618731934013219)
XLA Ops:
  7.2 0.7 all-gather.2.cloned.1.call-update
  8.0 0.7 compare_select_fusion
  8.8 1.1 multiply_reduce_fusion.1
  9.9 72.4 %all-gather.2.cloned.1.call-done = bf16[8192,256]{1,0:T(8,128)(2,1)} async-done(((bf16[512,256]{1,0:T(8,128)(2,1)}), bf16[8192,256]{1,0:T(8,128)(2,1)}) %all-gather.2.cloned.1.call-update) | async-done | bytes 4194320 | tf_op jit(solution)/shard_map/all_gather | solution.py:38
  82.4 5.0 %gather_fusion = bf16[64,128,256]{2,1,0:T(8,128)(2,1)} fusion(bf16[64,128,256]{2,1,0:T(8,128)(2,1)} %bitcast.66, s32[1024]{0:T(1024)S(1)} %pad_clamp_fusion), kind=kCustom, calls=%fused_computation | custom fusion | bytes 8388864 | tf_op jit(solution)/shard_map/gather | solution.py:43
  87.3 3.4 %multiply_reduce_fusion = f32[4,16,128]{2,1,0:T(8,128)S(1)} fusion(bf16[4,16,128,256]{3,2,1,0:T(8,128)(2,1)} %bitcast.64), kind=kLoop, calls=%fused_computation.2 | loop fusion | flops 6283264 | bytes 4227072 | tf_op jit(solution)/shard_map/reduce_sum | solution.py:45
  90.7 4.9 %fusion = f32[4,16,128,128]{3,2,1,0:T(8,128)} fusion(bf16[4,128,128,1]{2,1,3,0:T(8,128)(2,1)S(1)} %bitcast.62, bf16[4,16,128,256]{3,2,1,0:T(8,128)(2,1)} %bitcast.65, bf16[4,128,256,1]{2,1,3,0:T(8,128)(2,1)S(1)} %bitcast.68, f32[4,128]{1,0:T(4,128)S(1)} %bitcast.69, f32[4,16,128]{2,1,0:T(8,128)S(1)} %multiply_reduce_fusion), kind=kOutput, calls=%fused_computation.4 | convolution fusion | flops 811597824 | bytes 8816640 | tf_op jit(solution)/shard_map/jtab,jbv->jtav/dot_general | solution.py:49
  95.6 2.5 %broadcast_in_dim.4 = f32[64,128,128]{2,1,0:T(8,128)} broadcast(f32[]{:T(128)} %constant.43.clone.1), dimensions={} | broadcast | bytes 4194308 | tf_op jit(solution)/shard_map/broadcast_in_dim | solution.py:50
  98.1 13.6 %scatter_fusion = f32[64,128,128]{2,1,0:T(8,128)} fusion(f32[64,128,128]{2,1,0:T(8,128)} %broadcast_in_dim.4, s32[64]{0:T(128)S(1)} %fusion.15, f32[64,128,128]{2,1,0:T(8,128)} %bitcast.67), kind=kCustom, calls=%fused_computation.1 | custom fusion | flops 1048576 | bytes 12583168 | tf_op jit(solution)/shard_map/scatter-add | solution.py:51
  111.8 0.7 copy-done.2
  112.6 0.2 fusion.4
  112.9 0.6 fusion.19
  113.6 5.8 %cholesky.59 = f32[64,64]{1,0:T(8,128)S(1)} custom-call(f32[64,64]{1,0:T(8,128)S(1)} %fusion.9), custom_call_target="Cholesky" | custom-call | tf_op jit(solution)/shard_map/jit(cholesky)/cholesky | solution.py:57
  119.5 0.6 compare_reduce_fusion.2
  120.1 0.7 fusion.10
  120.8 1.9 collective-permute-start
  122.9 1.0 collective-permute-done
  124.2 5.8 %cholesky.70 = f32[64,64]{1,0:T(8,128)S(1)} custom-call(f32[64,64]{1,0:T(8,128)S(1)} %fusion.8), custom_call_target="Cholesky" | custom-call | tf_op jit(solution)/shard_map/jit(cholesky)/cholesky | solution.py:29
  130.0 0.6 compare_reduce_fusion.1
  130.7 0.7 select_bitcast_fusion.1
  131.3 3.3 %collective-permute-start.1 = (f32[64,64]{1,0:T(8,128)S(1)}, f32[64,64]{1,0:T(8,128)S(1)}, u32[]{:S(2)}, u32[]{:S(2)}) collective-permute-start(f32[64,64]{1,0:T(8,128)S(1)} %get-tuple-element.7), channel_id=1, source_target_pairs={{0,2},{1,3},{2,0},{3,1},{4,6},{5,7},{6,4},{7,5},{8,10},{9,11},{10,... | collective-permute-start | bytes 49160 | tf_op jit(solution)/shard_map/ppermute | solution.py:14
  134.7 4.9 %custom-call.6 = f32[1,64,64]{1,2,0:T(8,128)S(1)} custom-call(f32[1,64,64]{2,1,0:T(8,128)S(1)} %get-tuple-element.6), custom_call_target="InvertDiagBlocksLowerTriangular" | custom-call | tf_op jit(solution)/shard_map/triangular_solve/custom-call.0 | solution.py:30
  139.6 0.2 fusion.21
  139.8 0.2 convolution_bitcast_fusion.1
  140.3 5.8 %cholesky.81 = f32[64,64]{1,0:T(8,128)S(1)} custom-call(f32[64,64]{1,0:T(8,128)S(1)} %fusion.6), custom_call_target="Cholesky" | custom-call | tf_op jit(solution)/shard_map/jit(cholesky)/cholesky | solution.py:29
  146.2 0.6 compare_reduce_fusion
  146.8 0.7 select_bitcast_fusion
  147.5 4.9 %custom-call.7 = f32[1,64,64]{1,2,0:T(8,128)S(1)} custom-call(f32[1,64,64]{2,1,0:T(8,128)S(1)} %get-tuple-element.10), custom_call_target="InvertDiagBlocksLowerTriangular" | custom-call | tf_op jit(solution)/shard_map/triangular_solve/custom-call.0 | solution.py:30
  152.4 0.3 convolution_bitcast_fusion
  152.7 0.7 copy.15
  153.4 51.3 %reduce-scatter.2.cloned.1.call-done = f32[512,128]{1,0:T(8,128)} async-done(((f32[8192,128]{1,0:T(8,128)}), f32[512,128]{1,0:T(8,128)}) %reduce-scatter.2.cloned.1.call-update) | async-done | bytes 262160 | tf_op jit(solution)/shard_map/reduce_scatter | solution.py:52
  204.7 1.6 convert_element_type.20
  (27 shorter events, 1.3 us)
Async XLA Ops:
  7.2 83.6 %copy-start = (bf16[512,128]{1,0:T(8,128)(2,1)S(1)}, bf16[512,128]{1,0:T(8,128)(2,1)}, u32[]{:S(2)}) copy-start(bf16[512,128]{1,0:T(8,128)(2,1)} %param.8) | copy-start | bytes 393220
  7.2 75.2 %all-gather.2.cloned.1.call-start = ((), (), s32[]{:S(2)}) async-start(), calls=%async_computation.1 | async-start | bytes 4456448 | tf_op jit(solution)/shard_map/all_gather | solution.py:38
  7.9 196.8 %reduce-scatter.2.cloned.1.call-start = ((), (), s32[]{:S(2)}) async-start(), calls=%async_computation.2 | async-start | bytes 4456448 | tf_op jit(solution)/shard_map/reduce_scatter | solution.py:52
  87.3 3.4 %copy-start.1 = (bf16[512,256]{1,0:T(8,128)(2,1)S(1)}, bf16[512,256]{1,0:T(8,128)(2,1)}, u32[]{:S(2)}) copy-start(bf16[512,256]{1,0:T(8,128)(2,1)} %param.7) | copy-start | bytes 786436
  111.8 0.8 copy-start.2
  120.8 3.1 %collective-permute-start = (f32[64,64]{1,0:T(8,128)S(1)}, f32[64,64]{1,0:T(8,128)S(1)}, u32[]{:S(2)}, u32[]{:S(2)}) collective-permute-start(f32[64,64]{1,0:T(8,128)S(1)} %fusion.10), channel_id=1, source_target_pairs={{0,1},{1,0},{2,3},{3,2},{4,5},{5,4},{6,7},{7,6},{8,9},{9,8},{10,11... | collective-permute-start | bytes 49160 | tf_op jit(solution)/shard_map/ppermute | solution.py:14
  131.3 8.7 %collective-permute-start.1 = (f32[64,64]{1,0:T(8,128)S(1)}, f32[64,64]{1,0:T(8,128)S(1)}, u32[]{:S(2)}, u32[]{:S(2)}) collective-permute-start(f32[64,64]{1,0:T(8,128)S(1)} %get-tuple-element.7), channel_id=1, source_target_pairs={{0,2},{1,3},{2,0},{3,1},{4,6},{5,7},{6,4},{7,5},{8,10},{9,11},{10,... | collective-permute-start | bytes 49160 | tf_op jit(solution)/shard_map/ppermute | solution.py:14
Sparse Core Ops, SparseCore 0:
  11.0 71.2 all-gather.1
  111.9 92.7 reduce-scatter.1
where the time goes:
time: 214 us; the launch traced here: 213 us
  waiting for transfers between devices  125 us (58%)
  other arithmetic  51.9 us (24%)
  between operations  14.3 us (7%)
  local copies, waits for them, and re-layouts  9.3 us (4%)
  matrix products  6.97 us (3%)
  starting transfers between devices  5.31 us (2%)
    all_gather x1, waiting for transfers between devices, on_device(): gathered = lax.all_gather(points, 'row', axis=0, tiled=True)  72.4 us
    reduce_scatter x1, waiting for transfers between devices, on_device(): lax.psum_scatter(partial_value.reshape(group_count * BLK, NV), 'row', sca...  51.3 us
    scatter-add x1, other arithmetic, on_device(): partial_value.at[local_ids.reshape(-1)].add(contrib.reshape(-1, BLK, NV))  13.6 us
    another operation x6, other arithmetic, level_merge(): merged = jnp.linalg.cholesky(gram)  13 us
    another operation x4, other arithmetic, level_merge(): lax.linalg.triangular_solve(merged, lower_own, left_side=True, lower=True)  11.1 us
    another operation x3, other arithmetic, on_device(): jnp.linalg.cholesky(jnp.dot(far.T, far, precision=lax.Precision.HIGHEST))  6.52 us
    ppermute x2, starting transfers between devices, partner(): return lax.ppermute(value, axis, pairs)  5.24 us
    gather x1, local copies, waits for them, and re-layouts, on_device(): targets = tblocks[local_ids]  4.97 us
  transfers between devices with their start and end apart: 4, of which 3 were waited for; matrix products, arithmetic and copies ran while one was open for 17% of the time, Pallas kernels for 0%

commit v1 on v0

--- a/solution.py
+++ b/solution.py
@@ -35,7 +35,24 @@
     n_local = near_blocks.shape[0]
     group_count = n_local * lax.axis_size("row")
     base = lax.axis_index("col") * group_count
-    gathered = lax.all_gather(points, "row", axis=0, tiled=True)
+    devices, here, span = (lax.axis_size("row"), lax.axis_index("row"), points.shape[0])
+    right_2 = [(i, (i + 1) % devices) for i in range(devices)]
+    left_2 = [(i, (i - 1) % devices) for i in range(devices)]
+    filled = jnp.zeros((*points.shape[:0], devices * span, *points.shape[0 + 1 :]), points.dtype)
+    filled = lax.dynamic_update_slice_in_dim(filled, points, here * span, axis=0)
+    from_left = from_right = points
+    half = devices // 2
+    for hop in range(1, half + 1):
+        from_left = lax.ppermute(from_left, "row", right_2)
+        filled = lax.dynamic_update_slice_in_dim(
+            filled, from_left, (here - hop) % devices * span, axis=0
+        )
+        if hop < devices - half:
+            from_right = lax.ppermute(from_right, "row", left_2)
+            filled = lax.dynamic_update_slice_in_dim(
+                filled, from_right, (here + hop) % devices * span, axis=0
+            )
+    gathered = filled
     tblocks = gathered.reshape(group_count, BLK, DIM)
     local_ids = near_blocks - base
     sources = points.reshape(n_local, BLK, DIM)

time: 214 us -> 237 us (1.11)
  starting transfers between devices: 5.31 us -> 70.9 us
  waiting for transfers between devices: 125 us -> 68.3 us
  local copies, waits for them, and re-layouts: 9.3 us -> 23.2 us
    all_gather x1 -> x0, waiting for transfers between devices: 72.4 us -> none  [on_device(): gathered = lax.all_gather(points, 'row', axis=0, tiled=True)]
    ppermute x0 -> x15, starting transfers between devices: none -> 66.9 us  [the longest x7 50 us: on_device(): from_right = lax.ppermute(from_right, 'row', left_2)]
    ppermute x0 -> x15, waiting for transfers between devices: none -> 20.2 us  [the longest x8 20.2 us: on_device(): from_left = lax.ppermute(from_left, 'row', right_2)]
    dynamic_update_slice x0 -> x16, local copies, waits for them, and re-layouts: none -> 11.7 us  [the longest x8 5.81 us: on_device(): lax.dynamic_update_slice_in_dim(filled, from_left, (here - hop) % devices...]
    reduce_scatter x1, waiting for transfers between devices: 51.3 us -> 47.1 us  [on_device(): lax.psum_scatter(partial_value.reshape(group_count * BLK, NV), 'row', sca...]
  transfers between devices with their start and end apart: 4 -> 18, of which waited for: 3 -> 9; matrix products, arithmetic and copies ran while one was open for 17% -> 21% of each run, Pallas kernels for 0% -> 0%
where the time goes in v1:
time: 237 us; the launch traced here: 236 us
  starting transfers between devices  70.9 us (30%)
  waiting for transfers between devices  68.3 us (29%)
  other arithmetic  51.9 us (22%)
  local copies, waits for them, and re-layouts  23.2 us (10%)
  between operations  14.7 us (6%)
  matrix products  6.96 us (3%)
    ppermute x7, starting transfers between devices, on_device(): from_right = lax.ppermute(from_right, 'row', left_2)  50 us
    reduce_scatter x1, waiting for transfers between devices, on_device(): lax.psum_scatter(partial_value.reshape(group_count * BLK, NV), 'row', sca...  47.1 us
    ppermute x8, waiting for transfers between devices, on_device(): from_left = lax.ppermute(from_left, 'row', right_2)  20.2 us
    ppermute x8, starting transfers between devices, on_device(): from_left = lax.ppermute(from_left, 'row', right_2)  16.9 us
    scatter-add x1, other arithmetic, on_device(): partial_value.at[local_ids.reshape(-1)].add(contrib.reshape(-1, BLK, NV))  13.6 us
    another operation x6, other arithmetic, level_merge(): merged = jnp.linalg.cholesky(gram)  13 us
    another operation x4, other arithmetic, level_merge(): lax.linalg.triangular_solve(merged, lower_own, left_side=True, lower=True)  11.1 us
    another operation x3, other arithmetic, on_device(): jnp.linalg.cholesky(jnp.dot(far.T, far, precision=lax.Precision.HIGHEST))  6.52 us
  transfers between devices with their start and end apart: 18, of which 9 were waited for; matrix products, arithmetic and copies ran while one was open for 21% of the time, Pallas kernels for 0%

profile of v1, /device:TPU:2, one launch (start us, length us, event | category | flops | bytes accessed | tf_op | source)
XLA Modules:
  0.0 235.8 jit_solution(11581368593372789796)
XLA Ops:
  7.2 3.5 %collective-permute-start = (bf16[512,256]{1,0:T(8,128)(2,1)}, bf16[512,256]{1,0:T(8,128)(2,1)S(1)}, u32[]{:S(2)}, u32[]{:S(2)}) collective-permute-start(bf16[512,256]{1,0:T(8,128)(2,1)} %param.7), channel_id=1, source_target_pairs={{0,32},{32,64},{64,96},{96,128},{128,160},{160,192},{192,224},{224... | collective-permute-start | bytes 786440 | tf_op jit(solution)/shard_map/ppermute | solution.py:46
  10.8 6.3 %collective-permute-start.1 = (bf16[512,256]{1,0:T(8,128)(2,1)}, bf16[512,256]{1,0:T(8,128)(2,1)S(1)}, u32[]{:S(2)}, u32[]{:S(2)}) collective-permute-start(bf16[512,256]{1,0:T(8,128)(2,1)} %param.7), channel_id=1, source_target_pairs={{0,480},{32,0},{64,32},{96,64},{128,96},{160,128},{192,160},{224,1... | collective-permute-start | bytes 786440 | tf_op jit(solution)/shard_map/ppermute | solution.py:51
  17.1 2.6 %collective-permute-done = bf16[512,256]{1,0:T(8,128)(2,1)S(1)} collective-permute-done((bf16[512,256]{1,0:T(8,128)(2,1)}, bf16[512,256]{1,0:T(8,128)(2,1)S(1)}, u32[]{:S(2)}, u32[]{:S(2)}) %collective-permute-start) | collective-permute-done | bytes 262176 | tf_op jit(solution)/shard_map/ppermute | solution.py:46
  19.7 1.9 collective-permute-start.2
  22.4 7.2 %collective-permute-start.3 = (bf16[512,256]{1,0:T(8,128)(2,1)S(1)}, bf16[512,256]{1,0:T(8,128)(2,1)S(1)}, u32[]{:S(2)}, u32[]{:S(2)}) collective-permute-start(bf16[512,256]{1,0:T(8,128)(2,1)S(1)} %collective-permute-done.1), channel_id=1, source_target_pairs={{0,480},{32,0},{64,32},{96,64},{128,96},{160,128},{192,160},{224,1... | collective-permute-start | bytes 786440 | tf_op jit(solution)/shard_map/ppermute | solution.py:51
  31.3 1.9 collective-permute-start.4
  34.4 7.2 %collective-permute-start.5 = (bf16[512,256]{1,0:T(8,128)(2,1)S(1)}, bf16[512,256]{1,0:T(8,128)(2,1)S(1)}, u32[]{:S(2)}, u32[]{:S(2)}) collective-permute-start(bf16[512,256]{1,0:T(8,128)(2,1)S(1)} %collective-permute-done.3), channel_id=1, source_target_pairs={{0,480},{32,0},{64,32},{96,64},{128,96},{160,128},{192,160},{224,1... | collective-permute-start | bytes 786440 | tf_op jit(solution)/shard_map/ppermute | solution.py:51
  41.6 2.2 broadcast_in_dim.7
  44.6 1.9 collective-permute-start.6
  47.5 7.2 %collective-permute-start.7 = (bf16[512,256]{1,0:T(8,128)(2,1)S(1)}, bf16[512,256]{1,0:T(8,128)(2,1)S(1)}, u32[]{:S(2)}, u32[]{:S(2)}) collective-permute-start(bf16[512,256]{1,0:T(8,128)(2,1)S(1)} %collective-permute-done.5), channel_id=1, source_target_pairs={{0,480},{32,0},{64,32},{96,64},{128,96},{160,128},{192,160},{224,1... | collective-permute-start | bytes 786440 | tf_op jit(solution)/shard_map/ppermute | solution.py:51
  55.5 1.9 collective-permute-done.6
  57.4 1.9 collective-permute-start.8
  60.8 7.5 %collective-permute-start.9 = (bf16[512,256]{1,0:T(8,128)(2,1)S(1)}, bf16[512,256]{1,0:T(8,128)(2,1)S(1)}, u32[]{:S(2)}, u32[]{:S(2)}) collective-permute-start(bf16[512,256]{1,0:T(8,128)(2,1)S(1)} %collective-permute-done.7), channel_id=1, source_target_pairs={{0,480},{32,0},{64,32},{96,64},{128,96},{160,128},{192,160},{224,1... | collective-permute-start | bytes 786440 | tf_op jit(solution)/shard_map/ppermute | solution.py:51
  69.1 2.8 %collective-permute-done.8 = bf16[512,256]{1,0:T(8,128)(2,1)S(1)} collective-permute-done((bf16[512,256]{1,0:T(8,128)(2,1)S(1)}, bf16[512,256]{1,0:T(8,128)(2,1)S(1)}, u32[]{:S(2)}, u32[]{:S(2)}) %collective-permute-start.8) | collective-permute-done | bytes 262176 | tf_op jit(solution)/shard_map/ppermute | solution.py:46
  71.8 1.9 collective-permute-start.10
  75.2 7.4 %collective-permute-start.11 = (bf16[512,256]{1,0:T(8,128)(2,1)S(1)}, bf16[512,256]{1,0:T(8,128)(2,1)S(1)}, u32[]{:S(2)}, u32[]{:S(2)}) collective-permute-start(bf16[512,256]{1,0:T(8,128)(2,1)S(1)} %collective-permute-done.9), channel_id=1, source_target_pairs={{0,480},{32,0},{64,32},{96,64},{128,96},{160,128},{192,160},{224,1... | collective-permute-start | bytes 786440 | tf_op jit(solution)/shard_map/ppermute | solution.py:51
  83.4 2.4 %collective-permute-done.10 = bf16[512,256]{1,0:T(8,128)(2,1)S(1)} collective-permute-done((bf16[512,256]{1,0:T(8,128)(2,1)S(1)}, bf16[512,256]{1,0:T(8,128)(2,1)S(1)}, u32[]{:S(2)}, u32[]{:S(2)}) %collective-permute-start.10) | collective-permute-done | bytes 262176 | tf_op jit(solution)/shard_map/ppermute | solution.py:46
  89.2 7.0 %collective-permute-start.13 = (bf16[512,256]{1,0:T(8,128)(2,1)S(1)}, bf16[512,256]{1,0:T(8,128)(2,1)S(1)}, u32[]{:S(2)}, u32[]{:S(2)}) collective-permute-start(bf16[512,256]{1,0:T(8,128)(2,1)S(1)} %collective-permute-done.11), channel_id=1, source_target_pairs={{0,480},{32,0},{64,32},{96,64},{128,96},{160,128},{192,160},{224,1... | collective-permute-start | bytes 786440 | tf_op jit(solution)/shard_map/ppermute | solution.py:51
  102.7 7.2 %collective-permute-done.14 = bf16[512,256]{1,0:T(8,128)(2,1)S(1)} collective-permute-done((bf16[512,256]{1,0:T(8,128)(2,1)S(1)}, bf16[512,256]{1,0:T(8,128)(2,1)S(1)}, u32[]{:S(2)}, u32[]{:S(2)}) %collective-permute-start.14) | collective-permute-done | bytes 262176 | tf_op jit(solution)/shard_map/ppermute | solution.py:46
  110.6 5.0 %gather_fusion = bf16[64,128,256]{2,1,0:T(8,128)(2,1)} fusion(bf16[64,128,256]{2,1,0:T(8,128)(2,1)} %bitcast.1, s32[1024]{0:T(1024)S(1)} %pad_clamp_fusion), kind=kCustom, calls=%fused_computation | custom fusion | bytes 8388864 | tf_op jit(solution)/shard_map/gather | solution.py:60
  115.5 3.3 %multiply_reduce_fusion = f32[4,16,128]{2,1,0:T(8,128)S(1)} fusion(bf16[4,16,128,256]{3,2,1,0:T(8,128)(2,1)} %bitcast.64), kind=kLoop, calls=%fused_computation.2 | loop fusion | flops 6283264 | bytes 4227072 | tf_op jit(solution)/shard_map/reduce_sum | solution.py:62
  118.9 4.9 %fusion = f32[4,16,128,128]{3,2,1,0:T(8,128)} fusion(bf16[4,128,128,1]{2,1,3,0:T(8,128)(2,1)S(1)} %bitcast.62, bf16[4,16,128,256]{3,2,1,0:T(8,128)(2,1)} %bitcast.65, bf16[4,128,256,1]{2,1,3,0:T(8,128)(2,1)S(1)} %bitcast.67, f32[4,128]{1,0:T(4,128)S(1)} %bitcast.68, f32[4,16,128]{2,1,0:T(8,128)S(1)} %multiply_reduce_fusion), kind=kOutput, calls=%fused_computation.4 | convolution fusion | flops 811597824 | bytes 8816640 | tf_op jit(solution)/shard_map/jtab,jbv->jtav/dot_general | solution.py:66
  123.8 2.5 %broadcast_in_dim.6 = f32[64,128,128]{2,1,0:T(8,128)} broadcast(f32[]{:T(128)} %constant.132.clone.1), dimensions={} | broadcast | bytes 4194308 | tf_op jit(solution)/shard_map/broadcast_in_dim | solution.py:67
  126.3 13.6 %scatter_fusion = f32[64,128,128]{2,1,0:T(8,128)} fusion(f32[64,128,128]{2,1,0:T(8,128)} %broadcast_in_dim.6, s32[64]{0:T(128)S(1)} %fusion.15, f32[64,128,128]{2,1,0:T(8,128)} %bitcast.66), kind=kCustom, calls=%fused_computation.1 | custom fusion | flops 1048576 | bytes 12583168 | tf_op jit(solution)/shard_map/scatter-add | solution.py:68
  141.7 5.8 %cholesky.59 = f32[64,64]{1,0:T(8,128)S(1)} custom-call(f32[64,64]{1,0:T(8,128)S(1)} %fusion.9), custom_call_target="Cholesky" | custom-call | tf_op jit(solution)/shard_map/jit(cholesky)/cholesky | solution.py:74
  148.9 1.9 collective-permute-start.15
  152.3 5.8 %cholesky.70 = f32[64,64]{1,0:T(8,128)S(1)} custom-call(f32[64,64]{1,0:T(8,128)S(1)} %fusion.8), custom_call_target="Cholesky" | custom-call | tf_op jit(solution)/shard_map/jit(cholesky)/cholesky | solution.py:29
  159.5 2.1 collective-permute-start.16
  161.6 4.9 %custom-call.6 = f32[1,64,64]{1,2,0:T(8,128)S(1)} custom-call(f32[1,64,64]{2,1,0:T(8,128)S(1)} %get-tuple-element.6), custom_call_target="InvertDiagBlocksLowerTriangular" | custom-call | tf_op jit(solution)/shard_map/triangular_solve/custom-call.0 | solution.py:30
  167.2 5.8 %cholesky.81 = f32[64,64]{1,0:T(8,128)S(1)} custom-call(f32[64,64]{1,0:T(8,128)S(1)} %fusion.6), custom_call_target="Cholesky" | custom-call | tf_op jit(solution)/shard_map/jit(cholesky)/cholesky | solution.py:29
  174.4 4.9 %custom-call.7 = f32[1,64,64]{1,2,0:T(8,128)S(1)} custom-call(f32[1,64,64]{2,1,0:T(8,128)S(1)} %get-tuple-element.10), custom_call_target="InvertDiagBlocksLowerTriangular" | custom-call | tf_op jit(solution)/shard_map/triangular_solve/custom-call.0 | solution.py:30
  180.3 47.1 %reduce-scatter.2.cloned.1.call-done = f32[512,128]{1,0:T(8,128)} async-done(((f32[8192,128]{1,0:T(8,128)}), f32[512,128]{1,0:T(8,128)}) %reduce-scatter.2.cloned.1.call-update) | async-done | bytes 262160 | tf_op jit(solution)/shard_map/reduce_scatter | solution.py:69
  (71 shorter events, 31.2 us)
Async XLA Ops:
  7.2 111.7 %copy-start = (bf16[512,128]{1,0:T(8,128)(2,1)S(1)}, bf16[512,128]{1,0:T(8,128)(2,1)}, u32[]{:S(2)}) copy-start(bf16[512,128]{1,0:T(8,128)(2,1)} %param.8) | copy-start | bytes 393220
  7.2 36.6 %copy-start.1 = (bf16[512,256]{1,0:T(8,128)(2,1)S(1)}, bf16[512,256]{1,0:T(8,128)(2,1)}, u32[]{:S(2)}) copy-start(bf16[512,256]{1,0:T(8,128)(2,1)} %param.7) | copy-start | bytes 786436
  7.2 220.2 %reduce-scatter.2.cloned.1.call-start = ((), (), s32[]{:S(2)}) async-start(), calls=%async_computation.1 | async-start | bytes 4456448 | tf_op jit(solution)/shard_map/reduce_scatter | solution.py:69
  7.2 12.5 %collective-permute-start = (bf16[512,256]{1,0:T(8,128)(2,1)}, bf16[512,256]{1,0:T(8,128)(2,1)S(1)}, u32[]{:S(2)}, u32[]{:S(2)}) collective-permute-start(bf16[512,256]{1,0:T(8,128)(2,1)} %param.7), channel_id=1, source_target_pairs={{0,32},{32,64},{64,96},{96,128},{128,160},{160,192},{192,224},{224... | collective-permute-start | bytes 786440 | tf_op jit(solution)/shard_map/ppermute | solution.py:46
  10.8 11.7 %collective-permute-start.1 = (bf16[512,256]{1,0:T(8,128)(2,1)}, bf16[512,256]{1,0:T(8,128)(2,1)S(1)}, u32[]{:S(2)}, u32[]{:S(2)}) collective-permute-start(bf16[512,256]{1,0:T(8,128)(2,1)} %param.7), channel_id=1, source_target_pairs={{0,480},{32,0},{64,32},{96,64},{128,96},{160,128},{192,160},{224,1... | collective-permute-start | bytes 786440 | tf_op jit(solution)/shard_map/ppermute | solution.py:51
  19.7 11.6 %collective-permute-start.2 = (bf16[512,256]{1,0:T(8,128)(2,1)S(1)}, bf16[512,256]{1,0:T(8,128)(2,1)S(1)}, u32[]{:S(2)}, u32[]{:S(2)}) collective-permute-start(bf16[512,256]{1,0:T(8,128)(2,1)S(1)} %collective-permute-done), channel_id=1, source_target_pairs={{0,32},{32,64},{64,96},{96,128},{128,160},{160,192},{192,224},{224... | collective-permute-start | bytes 786440 | tf_op jit(solution)/shard_map/ppermute | solution.py:46
  22.4 11.9 %collective-permute-start.3 = (bf16[512,256]{1,0:T(8,128)(2,1)S(1)}, bf16[512,256]{1,0:T(8,128)(2,1)S(1)}, u32[]{:S(2)}, u32[]{:S(2)}) collective-permute-start(bf16[512,256]{1,0:T(8,128)(2,1)S(1)} %collective-permute-done.1), channel_id=1, source_target_pairs={{0,480},{32,0},{64,32},{96,64},{128,96},{160,128},{192,160},{224,1... | collective-permute-start | bytes 786440 | tf_op jit(solution)/shard_map/ppermute | solution.py:51
  31.3 13.3 %collective-permute-start.4 = (bf16[512,256]{1,0:T(8,128)(2,1)S(1)}, bf16[512,256]{1,0:T(8,128)(2,1)S(1)}, u32[]{:S(2)}, u32[]{:S(2)}) collective-permute-start(bf16[512,256]{1,0:T(8,128)(2,1)S(1)} %collective-permute-done.2), channel_id=1, source_target_pairs={{0,32},{32,64},{64,96},{96,128},{128,160},{160,192},{192,224},{224... | collective-permute-start | bytes 786440 | tf_op jit(solution)/shard_map/ppermute | solution.py:46
  34.4 13.2 %collective-permute-start.5 = (bf16[512,256]{1,0:T(8,128)(2,1)S(1)}, bf16[512,256]{1,0:T(8,128)(2,1)S(1)}, u32[]{:S(2)}, u32[]{:S(2)}) collective-permute-start(bf16[512,256]{1,0:T(8,128)(2,1)S(1)} %collective-permute-done.3), channel_id=1, source_target_pairs={{0,480},{32,0},{64,32},{96,64},{128,96},{160,128},{192,160},{224,1... | collective-permute-start | bytes 786440 | tf_op jit(solution)/shard_map/ppermute | solution.py:51
  44.6 12.8 %collective-permute-start.6 = (bf16[512,256]{1,0:T(8,128)(2,1)S(1)}, bf16[512,256]{1,0:T(8,128)(2,1)S(1)}, u32[]{:S(2)}, u32[]{:S(2)}) collective-permute-start(bf16[512,256]{1,0:T(8,128)(2,1)S(1)} %collective-permute-done.4), channel_id=1, source_target_pairs={{0,32},{32,64},{64,96},{96,128},{128,160},{160,192},{192,224},{224... | collective-permute-start | bytes 786440 | tf_op jit(solution)/shard_map/ppermute | solution.py:46
  47.5 13.3 %collective-permute-start.7 = (bf16[512,256]{1,0:T(8,128)(2,1)S(1)}, bf16[512,256]{1,0:T(8,128)(2,1)S(1)}, u32[]{:S(2)}, u32[]{:S(2)}) collective-permute-start(bf16[512,256]{1,0:T(8,128)(2,1)S(1)} %collective-permute-done.5), channel_id=1, source_target_pairs={{0,480},{32,0},{64,32},{96,64},{128,96},{160,128},{192,160},{224,1... | collective-permute-start | bytes 786440 | tf_op jit(solution)/shard_map/ppermute | solution.py:51
  57.4 14.4 %collective-permute-start.8 = (bf16[512,256]{1,0:T(8,128)(2,1)S(1)}, bf16[512,256]{1,0:T(8,128)(2,1)S(1)}, u32[]{:S(2)}, u32[]{:S(2)}) collective-permute-start(bf16[512,256]{1,0:T(8,128)(2,1)S(1)} %collective-permute-done.6), channel_id=1, source_target_pairs={{0,32},{32,64},{64,96},{96,128},{128,160},{160,192},{192,224},{224... | collective-permute-start | bytes 786440 | tf_op jit(solution)/shard_map/ppermute | solution.py:46
  60.8 14.4 %collective-permute-start.9 = (bf16[512,256]{1,0:T(8,128)(2,1)S(1)}, bf16[512,256]{1,0:T(8,128)(2,1)S(1)}, u32[]{:S(2)}, u32[]{:S(2)}) collective-permute-start(bf16[512,256]{1,0:T(8,128)(2,1)S(1)} %collective-permute-done.7), channel_id=1, source_target_pairs={{0,480},{32,0},{64,32},{96,64},{128,96},{160,128},{192,160},{224,1... | collective-permute-start | bytes 786440 | tf_op jit(solution)/shard_map/ppermute | solution.py:51
  71.8 14.0 %collective-permute-start.10 = (bf16[512,256]{1,0:T(8,128)(2,1)S(1)}, bf16[512,256]{1,0:T(8,128)(2,1)S(1)}, u32[]{:S(2)}, u32[]{:S(2)}) collective-permute-start(bf16[512,256]{1,0:T(8,128)(2,1)S(1)} %collective-permute-done.8), channel_id=1, source_target_pairs={{0,32},{32,64},{64,96},{96,128},{128,160},{160,192},{192,224},{224... | collective-permute-start | bytes 786440 | tf_op jit(solution)/shard_map/ppermute | solution.py:46
  75.2 14.0 %collective-permute-start.11 = (bf16[512,256]{1,0:T(8,128)(2,1)S(1)}, bf16[512,256]{1,0:T(8,128)(2,1)S(1)}, u32[]{:S(2)}, u32[]{:S(2)}) collective-permute-start(bf16[512,256]{1,0:T(8,128)(2,1)S(1)} %collective-permute-done.9), channel_id=1, source_target_pairs={{0,480},{32,0},{64,32},{96,64},{128,96},{160,128},{192,160},{224,1... | collective-permute-start | bytes 786440 | tf_op jit(solution)/shard_map/ppermute | solution.py:51
  85.8 12.7 %collective-permute-start.12 = (bf16[512,256]{1,0:T(8,128)(2,1)S(1)}, bf16[512,256]{1,0:T(8,128)(2,1)S(1)}, u32[]{:S(2)}, u32[]{:S(2)}) collective-permute-start(bf16[512,256]{1,0:T(8,128)(2,1)S(1)} %collective-permute-done.10), channel_id=1, source_target_pairs={{0,32},{32,64},{64,96},{96,128},{128,160},{160,192},{192,224},{224... | collective-permute-start | bytes 786440 | tf_op jit(solution)/shard_map/ppermute | solution.py:46
  89.2 12.7 %collective-permute-start.13 = (bf16[512,256]{1,0:T(8,128)(2,1)S(1)}, bf16[512,256]{1,0:T(8,128)(2,1)S(1)}, u32[]{:S(2)}, u32[]{:S(2)}) collective-permute-start(bf16[512,256]{1,0:T(8,128)(2,1)S(1)} %collective-permute-done.11), channel_id=1, source_target_pairs={{0,480},{32,0},{64,32},{96,64},{128,96},{160,128},{192,160},{224,1... | collective-permute-start | bytes 786440 | tf_op jit(solution)/shard_map/ppermute | solution.py:51
  98.5 11.3 %collective-permute-start.14 = (bf16[512,256]{1,0:T(8,128)(2,1)S(1)}, bf16[512,256]{1,0:T(8,128)(2,1)S(1)}, u32[]{:S(2)}, u32[]{:S(2)}) collective-permute-start(bf16[512,256]{1,0:T(8,128)(2,1)S(1)} %collective-permute-done.12), channel_id=1, source_target_pairs={{0,32},{32,64},{64,96},{96,128},{128,160},{160,192},{192,224},{224... | collective-permute-start | bytes 786440 | tf_op jit(solution)/shard_map/ppermute | solution.py:46
  139.9 0.8 copy-start.2
  148.9 3.1 %collective-permute-start.15 = (f32[64,64]{1,0:T(8,128)S(1)}, f32[64,64]{1,0:T(8,128)S(1)}, u32[]{:S(2)}, u32[]{:S(2)}) collective-permute-start(f32[64,64]{1,0:T(8,128)S(1)} %fusion.10), channel_id=1, source_target_pairs={{0,1},{1,0},{2,3},{3,2},{4,5},{5,4},{6,7},{7,6},{8,9},{9,8},{10,11... | collective-permute-start | bytes 49160 | tf_op jit(solution)/shard_map/ppermute | solution.py:14
  159.5 7.5 %collective-permute-start.16 = (f32[64,64]{1,0:T(8,128)S(1)}, f32[64,64]{1,0:T(8,128)S(1)}, u32[]{:S(2)}, u32[]{:S(2)}) collective-permute-start(f32[64,64]{1,0:T(8,128)S(1)} %get-tuple-element.7), channel_id=1, source_target_pairs={{0,2},{1,3},{2,0},{3,1},{4,6},{5,7},{6,4},{7,5},{8,10},{9,11},{10,... | collective-permute-start | bytes 49160 | tf_op jit(solution)/shard_map/ppermute | solution.py:14
Sparse Core Ops, SparseCore 0:
  140.1 87.2 reduce-scatter.1
